TPU v7x, 32 devices: a whole 2x2x4 slice. The times are simulated.
32 devices in a mesh: groups: 2 (over y), expert: 8 (over z, x), dp: 2 (over core).
Axes of the slice: x: 2, y: 2, z: 4, core: 2. Of those that a mesh axis runs over, the one named last changes fastest.
Arguments:
- normed: bfloat16 [672, 2048], P(('groups', 'expert'), 'dp'), parts along dimension 0, may hold values from -6 to 6
- cotangent: bfloat16 [672, 2048], P(('groups', 'expert'), 'dp'), parts along dimension 0, may hold values from -6 to 6
- expert_ids: int32 [672, 10], P(('groups', 'expert')), parts along dimension 0, may hold values from 0 to 23, all different within a row; in each aligned block of 42 rows (0 to 41, 42 to 83, ...) at most 28 rows name the same one
- route_weights: float32 [672, 10], P(('groups', 'expert')), parts along dimension 0, may hold values from 0.02 to 0.6
- w_gate: bfloat16 [24, 2048, 512], P('expert', 'dp'), may hold values from -0.125 to 0.125
- w_up: bfloat16 [24, 2048, 512], P('expert', 'dp'), may hold values from -0.125 to 0.125
- w_down: bfloat16 [24, 512, 2048], P('expert', None, 'dp'), may hold values from -0.25 to 0.25
Outputs:
- moe_out: bfloat16 [672, 2048], P(('groups', 'expert'), 'dp'), parts along dimension 0
- grad_normed: bfloat16 [672, 2048], P(('groups', 'expert'), 'dp'), parts along dimension 0
- grad_gate: bfloat16 [48, 2048, 512], P(('groups', 'expert'), 'dp'), parts along dimension 0
- grad_up: bfloat16 [48, 2048, 512], P(('groups', 'expert'), 'dp'), parts along dimension 0
- grad_down: bfloat16 [48, 512, 2048], P(('groups', 'expert'), None, 'dp'), parts along dimension 0
There are 2 independent parts, one for each index of `groups`. A program takes and returns all parts, laid end to end along the dimension named above; an argument that names none is the same for every part. Nothing has to cross between parts.
Inputs may be any that keep to these rules, and one draw needn't show every extreme that they name: `expert_ids`: each row names 10 different experts. Among the rows of one index of expert (aligned blocks of 42 rows) no expert is named by more than 28 rows, and in every draw some expert is named by exactly 28 rows of some block.
All inputs are finite; a program needn't handle non-finite values.
Results may differ from a plain program's by a relative error of at most 0.0064.
Values may be sent and summed in bfloat16 or wider, within the bound.
A program may use at most 128 MiB of HBM per device.

v0:
```python
import jax
import jax.numpy as jnp
from jax import lax
from jax.sharding import PartitionSpec as P


def shards(normed, cotangent, expert_ids, route_weights, w_gate, w_up, w_down):
    tok_rows, width = normed.shape
    topk = expert_ids.shape[1]
    count_dev = lax.axis_size("expert")
    local_experts = w_gate.shape[0]
    experts = local_experts * count_dev
    slots = min(tok_rows, 8 * tok_rows * topk // (5 * experts))
    assigned = tok_rows * topk
    flat_ids = expert_ids.reshape(assigned)
    onehot = (flat_ids[:, None] == jnp.arange(experts, dtype=jnp.int32)[None, :]).astype(jnp.int32)
    ranks = jnp.sum(onehot * jnp.cumsum(onehot, axis=0), axis=1) - 1
    owner = flat_ids // local_experts
    local_slot = flat_ids % local_experts
    gate_all, up_all, down_all = (w_gate, w_up, w_down)
    slot_of = (owner * local_experts + local_slot) * slots + ranks
    table = jnp.full((count_dev * local_experts * slots,), assigned, jnp.int32)
    table = table.at[slot_of].set(jnp.arange(assigned, dtype=jnp.int32))
    token_of = jnp.where(table < assigned, table // topk, tok_rows)
    scaled = (route_weights[:, :, None] * cotangent[:, None, :].astype(jnp.float32)).astype(
        jnp.bfloat16
    )
    scaled = scaled.reshape(assigned, width)
    x_padded = jnp.concatenate([normed, jnp.zeros((1, width), jnp.bfloat16)], axis=0)
    g_padded = jnp.concatenate([scaled, jnp.zeros((1, width), jnp.bfloat16)], axis=0)
    send_rows = x_padded[token_of].reshape(count_dev, local_experts, slots, width)
    send_grads = g_padded[table].reshape(count_dev, local_experts, slots, width)
    recv_rows, recv_grads = (
        lax.all_to_all(send_rows, "expert", split_axis=0, concat_axis=2, tiled=True),
        lax.all_to_all(send_grads, "expert", split_axis=0, concat_axis=2, tiled=True),
    )
    rows = recv_rows[0]
    grads = recv_grads[0]
    part_gate = jnp.einsum("jrd,jdf->jrf", rows, gate_all, preferred_element_type=jnp.float32)
    part_up = jnp.einsum("jrd,jdf->jrf", rows, up_all, preferred_element_type=jnp.float32)
    part_grad = jnp.einsum("jrd,jfd->jrf", grads, down_all, preferred_element_type=jnp.float32)
    pre_gate, pre_up = lax.psum((part_gate, part_up), "dp")
    sig = jax.nn.sigmoid(pre_gate)
    hidden = (pre_gate * sig * pre_up).astype(jnp.bfloat16)
    hidden_grad = lax.psum(part_grad, "dp")
    gate_grad = (hidden_grad * pre_up * sig * (1.0 + pre_gate * (1.0 - sig))).astype(jnp.bfloat16)
    up_grad = (hidden_grad * pre_gate * sig).astype(jnp.bfloat16)
    out_rows = jnp.einsum(
        "jrf,jfd->jrd", hidden, down_all, preferred_element_type=jnp.float32
    ).astype(jnp.bfloat16)
    row_grad = (
        jnp.einsum("jrf,jdf->jrd", gate_grad, gate_all, preferred_element_type=jnp.float32)
        + jnp.einsum("jrf,jdf->jrd", up_grad, up_all, preferred_element_type=jnp.float32)
    ).astype(jnp.bfloat16)
    sum_gate = jnp.einsum("jrd,jrf->jdf", rows, gate_grad, preferred_element_type=jnp.float32)
    sum_up = jnp.einsum("jrd,jrf->jdf", rows, up_grad, preferred_element_type=jnp.float32)
    sum_down = jnp.einsum("jrf,jrd->jfd", hidden, grads, preferred_element_type=jnp.float32)
    grad_gate = sum_gate.astype(jnp.bfloat16)
    grad_up = sum_up.astype(jnp.bfloat16)
    grad_down = sum_down.astype(jnp.bfloat16)
    back_out, back_grad = (
        lax.all_to_all(out_rows[None], "expert", split_axis=2, concat_axis=0, tiled=True),
        lax.all_to_all(row_grad[None], "expert", split_axis=2, concat_axis=0, tiled=True),
    )
    back_out = back_out.reshape(count_dev * local_experts * slots, width)[slot_of]
    back_grad = back_grad.reshape(count_dev * local_experts * slots, width)[slot_of]
    moe_out = jnp.sum(
        route_weights[:, :, None] * back_out.reshape(tok_rows, topk, width).astype(jnp.float32),
        axis=1,
    )
    grad_normed = jnp.sum(back_grad.reshape(tok_rows, topk, width).astype(jnp.float32), axis=1)
    return (
        moe_out.astype(jnp.bfloat16),
        grad_normed.astype(jnp.bfloat16),
        grad_gate,
        grad_up,
        grad_down,
    )


def solution(mesh):
    in_specs = (
        P(("groups", "expert"), "dp"),
        P(("groups", "expert"), "dp"),
        P(("groups", "expert"), None),
        P(("groups", "expert"), None),
        P("expert", "dp", None),
        P("expert", "dp", None),
        P("expert", None, "dp"),
    )
    out_specs = (
        P(("groups", "expert"), "dp"),
        P(("groups", "expert"), "dp"),
        P(("groups", "expert"), "dp", None),
        P(("groups", "expert"), "dp", None),
        P(("groups", "expert"), None, "dp"),
    )
    return jax.shard_map(shards, mesh=mesh, in_specs=in_specs, out_specs=out_specs, check_vma=False)
```

profile of v0, /device:TPU:0, one launch (start us, length us, event | category | flops | bytes accessed | tf_op | source)
XLA Modules:
  0.0 269.1 jit_solution(12380181924497505001)
XLA Ops:
  12.1 2.9 %scatter_custom_fusion = s32[672]{0:T(1024)S(1)} fusion(s32[420]{0:T(512)S(1)} %bitcast.57, s32[420]{0:T(512)S(1)} %iota.8, s32[]{:T(128)} %constant.24.clone.1), kind=kCustom, calls=%fused_computation.46 | custom fusion | bytes 2692 | tf_op jit(solution)/shard_map/scatter | solution.py:23
  15.9 3.5 %gather_fusion = bf16[672,1024]{1,0:T(8,128)(2,1)} fusion(bf16[43,1024]{1,0:T(8,128)(2,1)S(1)} %concatenate.6, s32[1024]{0:T(1024)S(1)} %get-tuple-element.16), kind=kCustom, calls=%fused_computation | custom fusion | bytes 2755200 | tf_op jit(solution)/shard_map/gather | solution.py:31
  19.4 3.1 %reshape.145 = bf16[8,3,28,1024]{3,2,1,0:T(8,128)(2,1)} reshape(bf16[672,1024]{1,0:T(8,128)(2,1)} %gather_fusion) | data formatting | bytes 2752512 | tf_op jit(solution)/shard_map/reshape | solution.py:31
  22.5 7.4 %all-to-all-start = ((bf16[8,3,28,1024]{3,2,1,0:T(8,128)(2,1)}), bf16[8,3,28,1024]{3,2,1,0:T(8,128)(2,1)}, u32[]{:S(2)}, u32[]{:S(2)}) async-start(bf16[8,3,28,1024]{3,2,1,0:T(8,128)(2,1)} %reshape.145), calls=%async_computation | async-start | bytes 3145728 | tf_op jit(solution)/shard_map/all_to_all | solution.py:34
  32.0 3.2 %mul.88 = f32[420,1024]{1,0:T(8,128)} reshape(f32[42,10,1024]{2,1,0:T(8,128)} %mul.87) | data formatting | bytes 3440640 | tf_op jit(solution)/shard_map/mul | solution.py:25
  37.7 5.8 %gather_fusion.2 = bf16[672,1024]{1,0:T(8,128)(2,1)} fusion(bf16[421,1024]{1,0:T(8,128)(2,1)} %concatenate.7, s32[1024]{0:T(1024)S(1)} %get-tuple-element.15), kind=kCustom, calls=%fused_computation.2 | custom fusion | bytes 2755200 | tf_op jit(solution)/shard_map/gather | solution.py:32
  43.5 3.1 %reshape.147 = bf16[8,3,28,1024]{3,2,1,0:T(8,128)(2,1)} reshape(bf16[672,1024]{1,0:T(8,128)(2,1)} %gather_fusion.2) | data formatting | bytes 2752512 | tf_op jit(solution)/shard_map/reshape | solution.py:32
  46.5 20.4 %all-to-all-done = bf16[8,3,28,1024]{3,2,1,0:T(8,128)(2,1)} async-done(((bf16[8,3,28,1024]{3,2,1,0:T(8,128)(2,1)}), bf16[8,3,28,1024]{3,2,1,0:T(8,128)(2,1)}, u32[]{:S(2)}, u32[]{:S(2)}) %all-to-all-start) | async-done | bytes 1376288 | tf_op jit(solution)/shard_map/all_to_all | solution.py:34
  67.0 4.3 %all-to-all-start.2 = ((bf16[8,3,28,1024]{3,2,1,0:T(8,128)(2,1)}), bf16[8,3,28,1024]{3,2,1,0:T(8,128)(2,1)}, u32[]{:S(2)}, u32[]{:S(2)}) async-start(bf16[8,3,28,1024]{3,2,1,0:T(8,128)(2,1)} %reshape.147), calls=%async_computation.2 | async-start | bytes 3145728 | tf_op jit(solution)/shard_map/all_to_all | solution.py:35
  71.3 2.7 %copy.36 = bf16[1,3,8,28,1024]{4,3,2,1,0:T(8,128)(2,1)} copy(bf16[1,3,8,28,1024]{4,3,1,2,0:T(8,128)(2,1)} %bitcast.4) | data formatting | bytes 2752512 | tf_op jit(solution)/shard_map/all_to_all | solution.py:34
  74.1 3.1 %squeeze.6 = bf16[3,224,1024]{2,1,0:T(8,128)(2,1)} reshape(bf16[1,3,8,28,1024]{4,3,2,1,0:T(8,128)(2,1)} %copy.36) | data formatting | bytes 2752512 | tf_op jit(solution)/shard_map/squeeze | solution.py:37
  77.2 4.4 %fusion.9 = f32[3,224,512]{2,1,0:T(8,128)} fusion(bf16[3,224,1024]{2,1,0:T(8,128)(2,1)} %squeeze.6, bf16[3,1024,512]{2,1,0:T(8,128)(2,1)} %param.12), kind=kOutput, calls=%fused_computation.50 | convolution fusion | flops 704643072 | bytes 5898240 | tf_op jit(solution)/shard_map/jrd,jdf->jrf/dot_general | solution.py:40
  83.6 24.3 %all-to-all-done.2 = bf16[8,3,28,1024]{3,2,1,0:T(8,128)(2,1)} async-done(((bf16[8,3,28,1024]{3,2,1,0:T(8,128)(2,1)}), bf16[8,3,28,1024]{3,2,1,0:T(8,128)(2,1)}, u32[]{:S(2)}, u32[]{:S(2)}) %all-to-all-start.2) | async-done | bytes 1376288 | tf_op jit(solution)/shard_map/all_to_all | solution.py:35
  107.9 2.7 %copy.41 = bf16[1,3,8,28,1024]{4,3,2,1,0:T(8,128)(2,1)} copy(bf16[1,3,8,28,1024]{4,3,1,2,0:T(8,128)(2,1)} %bitcast.9) | data formatting | bytes 2752512 | tf_op jit(solution)/shard_map/all_to_all | solution.py:35
  110.6 3.1 %squeeze.7 = bf16[3,224,1024]{2,1,0:T(8,128)(2,1)} reshape(bf16[1,3,8,28,1024]{4,3,2,1,0:T(8,128)(2,1)} %copy.41) | data formatting | bytes 2752512 | tf_op jit(solution)/shard_map/squeeze | solution.py:38
  113.8 3.5 %fusion.10 = f32[3,224,512]{2,1,0:T(8,128)} fusion(bf16[3,224,1024]{2,1,0:T(8,128)(2,1)} %squeeze.7, bf16[3,512,1024]{2,1,0:T(8,128)(2,1)S(1)} %copy-done), kind=kOutput, calls=%fused_computation.51 | convolution fusion | flops 704643072 | bytes 5898240 | tf_op jit(solution)/shard_map/jrd,jfd->jrf/dot_general | solution.py:41
  117.3 27.8 %all-reduce.6.cloned.1.call-done = (f32[3,224,512]{2,1,0:T(8,128)}, f32[3,224,512]{2,1,0:T(8,128)}, f32[3,224,512]{2,1,0:T(8,128)}) async-done(((f32[3,224,512]{2,1,0:T(8,128)}, f32[3,224,512]{2,1,0:T(8,128)}, f32[3,224,512]{2,1,0:T(8,128)}), (f32[3,224,512]{2,1,0:T(8,128)}, f32[3,224,512]{2,1,0:T(8,128)}, f32[3,224,512]{2,1,0:T(8,128)})) %all-reduce.6.cloned.1.call-update) | async-done | bytes 4128784 | tf_op jit(solution)/shard_map/psum | solution.py:42
  145.1 4.1 %multiply_convert_fusion.1 = (bf16[3,224,512]{2,1,0:T(8,128)(2,1)}, bf16[3,224,512]{2,1,0:T(8,128)(2,1)}, bf16[3,224,512]{2,1,0:T(8,128)(2,1)S(1)}) fusion(f32[3,224,512]{2,1,0:T(8,128)} %get-tuple-element.7, f32[3,224,512]{2,1,0:T(8,128)} %get-tuple-element.6, f32[3,224,512]{2,1,0:T(8,128)} %get-tuple-element.5), kind=kLoop, calls=%fused_computation.16 | loop fusion | flops 5505024 | bytes 6193152 | tf_op jit(solution)/shard_map/convert_element_type | solution.py:47
  150.2 2.4 copy.37
  152.6 6.0 %all-to-all-start.1 = ((bf16[1,3,224,1024]{3,1,0,2:T(4,128)(2,1)}), bf16[1,3,224,1024]{3,1,0,2:T(4,128)(2,1)}, u32[]{:S(2)}, u32[]{:S(2)}) async-start(bf16[1,3,224,1024]{3,1,0,2:T(4,128)(2,1)} %copy.37), calls=%async_computation.1 | async-start | bytes 3670016 | tf_op jit(solution)/shard_map/all_to_all | solution.py:62
  158.7 2.3 fusion.11
  162.2 2.4 copy.42
  164.6 37.3 %all-to-all-done.1 = bf16[1,3,224,1024]{3,1,0,2:T(4,128)(2,1)} async-done(((bf16[1,3,224,1024]{3,1,0,2:T(4,128)(2,1)}), bf16[1,3,224,1024]{3,1,0,2:T(4,128)(2,1)}, u32[]{:S(2)}, u32[]{:S(2)}) %all-to-all-start.1) | async-done | bytes 1376288 | tf_op jit(solution)/shard_map/all_to_all | solution.py:62
  201.9 4.3 %all-to-all-start.3 = ((bf16[1,3,224,1024]{3,1,0,2:T(4,128)(2,1)}), bf16[1,3,224,1024]{3,1,0,2:T(4,128)(2,1)}, u32[]{:S(2)}, u32[]{:S(2)}) async-start(bf16[1,3,224,1024]{3,1,0,2:T(4,128)(2,1)} %copy.42), calls=%async_computation.3 | async-start | bytes 3670016 | tf_op jit(solution)/shard_map/all_to_all | solution.py:63
  206.2 3.9 %convolution_convert_fusion = bf16[3,512,1024]{2,1,0:T(8,128)(2,1)} fusion(bf16[3,224,512]{2,1,0:T(8,128)(2,1)} %copy-done.8, bf16[3,224,1024]{2,1,0:T(8,128)(2,1)S(1)} %copy-done.7), kind=kOutput, calls=%fused_computation.7 | convolution fusion | flops 706215936 | bytes 5210112 | tf_op jit(solution)/shard_map/jrf,jrd->jfd/dot_general | solution.py:57
  210.2 2.8 %convolution_convert_fusion.1 = bf16[3,1024,512]{2,1,0:T(8,128)(2,1)} fusion(bf16[3,224,1024]{2,1,0:T(8,128)(2,1)S(1)} %copy-done.3, bf16[3,224,512]{2,1,0:T(8,128)(2,1)S(1)} %copy-done.11), kind=kOutput, calls=%fused_computation.8 | convolution fusion | flops 706215936 | bytes 5210112 | tf_op jit(solution)/shard_map/jrd,jrf->jdf/dot_general | solution.py:56
  213.0 2.8 %convolution_convert_fusion.2 = bf16[3,1024,512]{2,1,0:T(8,128)(2,1)} fusion(bf16[3,224,1024]{2,1,0:T(8,128)(2,1)S(1)} %copy-done.3, bf16[3,224,512]{2,1,0:T(8,128)(2,1)S(1)} %copy-done.9), kind=kOutput, calls=%fused_computation.9 | convolution fusion | flops 706215936 | bytes 5210112 | tf_op jit(solution)/shard_map/jrd,jrf->jdf/dot_general | solution.py:55
  218.2 2.7 %gather_fusion.1 = bf16[420,1024]{1,0:T(8,128)(2,1)} fusion(bf16[672,1024]{1,0:T(8,128)(2,1)S(1)} %reshape.146, s32[1024]{0:T(1024)S(1)} %pad_clamp_fusion.1), kind=kCustom, calls=%fused_computation.1 | custom fusion | bytes 1722000 | tf_op jit(solution)/shard_map/gather | solution.py:65
  224.2 24.3 %all-to-all-done.3 = bf16[1,3,224,1024]{3,1,0,2:T(4,128)(2,1)} async-done(((bf16[1,3,224,1024]{3,1,0,2:T(4,128)(2,1)}), bf16[1,3,224,1024]{3,1,0,2:T(4,128)(2,1)}, u32[]{:S(2)}, u32[]{:S(2)}) %all-to-all-start.3) | async-done | bytes 1376288 | tf_op jit(solution)/shard_map/all_to_all | solution.py:63
  251.9 5.1 %gather_fusion.3 = bf16[420,1024]{1,0:T(8,128)(2,1)} fusion(bf16[672,1024]{1,0:T(8,128)(2,1)} %reshape.148, s32[1024]{0:T(1024)S(1)} %pad_clamp_fusion.1), kind=kCustom, calls=%fused_computation.3 | custom fusion | bytes 1722000 | tf_op jit(solution)/shard_map/gather | solution.py:66
  257.0 2.6 reshape.149
  259.7 2.6 reduce_sum.32
  (71 shorter events, 23.7 us)
Async XLA Ops:
  7.2 106.6 %copy-start = (bf16[3,512,1024]{2,1,0:T(8,128)(2,1)S(1)}, bf16[3,512,1024]{2,1,0:T(8,128)(2,1)}, u32[]{:S(2)}) copy-start(bf16[3,512,1024]{2,1,0:T(8,128)(2,1)} %param.13) | copy-start | bytes 9437188
  22.5 7.4 %copy-start.13 = (f32[42,10]{0,1:T(8,128)S(1)}, f32[42,10]{0,1:T(8,128)}, u32[]{:S(2)}) copy-start(f32[42,10]{0,1:T(8,128)} %param.10) | copy-start | bytes 5044
  22.5 7.6 %copy-start.12 = (bf16[42,1024]{1,0:T(8,128)(2,1)S(1)}, bf16[42,1024]{1,0:T(8,128)(2,1)}, u32[]{:S(2)}) copy-start(bf16[42,1024]{1,0:T(8,128)(2,1)} %param.8) | copy-start | bytes 258052
  22.5 44.5 %all-to-all-start = ((bf16[8,3,28,1024]{3,2,1,0:T(8,128)(2,1)}), bf16[8,3,28,1024]{3,2,1,0:T(8,128)(2,1)}, u32[]{:S(2)}, u32[]{:S(2)}) async-start(bf16[8,3,28,1024]{3,2,1,0:T(8,128)(2,1)} %reshape.145), calls=%async_computation | async-start | bytes 3145728 | tf_op jit(solution)/shard_map/all_to_all | solution.py:34
  67.0 40.9 %all-to-all-start.2 = ((bf16[8,3,28,1024]{3,2,1,0:T(8,128)(2,1)}), bf16[8,3,28,1024]{3,2,1,0:T(8,128)(2,1)}, u32[]{:S(2)}, u32[]{:S(2)}) async-start(bf16[8,3,28,1024]{3,2,1,0:T(8,128)(2,1)} %reshape.147), calls=%async_computation.2 | async-start | bytes 3145728 | tf_op jit(solution)/shard_map/all_to_all | solution.py:35
  71.3 73.9 %all-reduce.6.cloned.1.call-start = ((), (), s32[]{:S(2)}) async-start(), calls=%async_computation.4 | async-start | bytes 8257536 | tf_op jit(solution)/shard_map/psum | solution.py:42
  77.2 4.4 %copy-start.2 = (bf16[3,224,1024]{2,1,0:T(8,128)(2,1)S(1)}, bf16[3,224,1024]{2,1,0:T(8,128)(2,1)}, u32[]{:S(2)}) copy-start(bf16[3,224,1024]{2,1,0:T(8,128)(2,1)} %squeeze.6) | copy-start | bytes 4128772
  77.2 4.4 %copy-start.4 = (bf16[3,1024,512]{2,1,0:T(8,128)(2,1)S(1)}, bf16[3,1024,512]{2,1,0:T(8,128)(2,1)}, u32[]{:S(2)}) copy-start(bf16[3,1024,512]{2,1,0:T(8,128)(2,1)} %param.11) | copy-start | bytes 9437188
  149.3 0.9 copy-start.8
  152.6 6.1 %copy-start.5 = (bf16[3,1024,512]{2,1,0:T(8,128)(2,1)S(1)}, bf16[3,1024,512]{2,1,0:T(8,128)(2,1)}, u32[]{:S(2)}) copy-start(bf16[3,1024,512]{2,1,0:T(8,128)(2,1)} %param.11) | copy-start | bytes 9437188
  152.6 49.2 %all-to-all-start.1 = ((bf16[1,3,224,1024]{3,1,0,2:T(4,128)(2,1)}), bf16[1,3,224,1024]{3,1,0,2:T(4,128)(2,1)}, u32[]{:S(2)}, u32[]{:S(2)}) async-start(bf16[1,3,224,1024]{3,1,0,2:T(4,128)(2,1)} %copy.37), calls=%async_computation.1 | async-start | bytes 3670016 | tf_op jit(solution)/shard_map/all_to_all | solution.py:62
  158.7 2.4 copy-start.6
  158.7 2.4 copy-start.10
  164.6 41.6 %copy-start.7 = (bf16[3,224,1024]{2,1,0:T(8,128)(2,1)S(1)}, bf16[3,224,1024]{2,1,0:T(8,128)(2,1)}, u32[]{:S(2)}) copy-start(bf16[3,224,1024]{2,1,0:T(8,128)(2,1)} %squeeze.7) | copy-start | bytes 4128772
  201.9 46.6 %all-to-all-start.3 = ((bf16[1,3,224,1024]{3,1,0,2:T(4,128)(2,1)}), bf16[1,3,224,1024]{3,1,0,2:T(4,128)(2,1)}, u32[]{:S(2)}, u32[]{:S(2)}) async-start(bf16[1,3,224,1024]{3,1,0,2:T(4,128)(2,1)} %copy.42), calls=%async_computation.3 | async-start | bytes 3670016 | tf_op jit(solution)/shard_map/all_to_all | solution.py:63
  206.2 4.0 %copy-start.3 = (bf16[3,224,1024]{2,1,0:T(8,128)(2,1)S(1)}, bf16[3,224,1024]{2,1,0:T(8,128)(2,1)}, u32[]{:S(2)}) copy-start(bf16[3,224,1024]{2,1,0:T(8,128)(2,1)} %squeeze.6) | copy-start | bytes 4128772
  206.2 4.0 %copy-start.11 = (bf16[3,224,512]{2,1,0:T(8,128)(2,1)S(1)}, bf16[3,224,512]{2,1,0:T(8,128)(2,1)}, u32[]{:S(2)}) copy-start(bf16[3,224,512]{2,1,0:T(8,128)(2,1)} %get-tuple-element.8) | copy-start | bytes 2064388
  210.2 2.8 %copy-start.9 = (bf16[3,224,512]{2,1,0:T(8,128)(2,1)S(1)}, bf16[3,224,512]{2,1,0:T(8,128)(2,1)}, u32[]{:S(2)}) copy-start(bf16[3,224,512]{2,1,0:T(8,128)(2,1)} %get-tuple-element.9) | copy-start | bytes 2064388
  251.9 10.3 %copy-start.1 = (bf16[3,512,1024]{2,1,0:T(8,128)(2,1)S(1)}, bf16[3,512,1024]{2,1,0:T(8,128)(2,1)}, u32[]{:S(2)}) copy-start(bf16[3,512,1024]{2,1,0:T(8,128)(2,1)} %param.13) | copy-start | bytes 9437188
Sparse Core Ops, SparseCore 0:
  117.4 27.6 all-reduce.5
where the time goes:
time: 270 us; the launch traced here: 269 us
  waiting for transfers between devices  134 us (50%)
  local copies, waits for them, and re-layouts  62.2 us (23%)
  matrix products  23.8 us (9%)
  starting transfers between devices  22.1 us (8%)
  between operations  14.3 us (5%)
  other arithmetic  12.6 us (5%)
    all_to_all x1, waiting for transfers between devices, shards(): lax.all_to_all(out_rows[None], 'expert', split_axis=2, concat_axis=0, til...  37.3 us
    psum x1, waiting for transfers between devices, shards(): pre_gate, pre_up = lax.psum((part_gate, part_up), 'dp')  27.8 us
    all_to_all x1, waiting for transfers between devices, shards(): lax.all_to_all(send_grads, 'expert', split_axis=0, concat_axis=2, tiled=T...  24.3 us
    all_to_all x1, waiting for transfers between devices, shards(): lax.all_to_all(row_grad[None], 'expert', split_axis=2, concat_axis=0, til...  24.3 us
    all_to_all x1, waiting for transfers between devices, shards(): lax.all_to_all(send_rows, 'expert', split_axis=0, concat_axis=2, tiled=True)  20.4 us
    all_to_all x1, starting transfers between devices, shards(): lax.all_to_all(send_rows, 'expert', split_axis=0, concat_axis=2, tiled=True)  7.38 us
    all_to_all x1, starting transfers between devices, shards(): lax.all_to_all(out_rows[None], 'expert', split_axis=2, concat_axis=0, til...  6.05 us
    gather x1, local copies, waits for them, and re-layouts, shards(): send_grads = g_padded[table].reshape(count_dev, local_experts, slots, width)  5.75 us
  transfers between devices with their start and end apart: 5, of which 5 were waited for; matrix products, arithmetic and copies ran while one was open for 20% of the time, Pallas kernels for 0%

commit v1 on v0

v1 whole, which is shorter than its diff:
```python
import functools

import jax
import jax.numpy as jnp
from jax import lax
from jax.experimental import pallas as pl
from jax.experimental.pallas import tpu as pltpu
from jax.sharding import PartitionSpec as P

F32, BF16 = jnp.float32, jnp.bfloat16
NN = (((1,), (0,)), ((), ()))
NT = (((1,), (1,)), ((), ()))
TN = (((0,), (0,)), ((), ()))
MESH = pl.DeviceIdType.MESH


def dot(a, b, dims):
    return lax.dot_general(a, b, dims, preferred_element_type=F32)


def kernel(n, rows, width, experts, x_in, c_in, wg_hbm, wu_hbm, wd_hbm,
           moe_ref, gn_ref, gg_hbm, gu_hbm, gd_hbm,
           xs, cs, xt, wg, wu, wd, own, snd, rcv, hid, gat, upg, part, red_out, red_in,
           out_g, out_u, out_d,
           w_sem, g_send, g_recv, d_send, d_recv, r_send, r_recv, o_sem):
    half = n // 2
    local = wg.shape[0]
    me_g, me_e, me_d = lax.axis_index("groups"), lax.axis_index("expert"), lax.axis_index("dp")
    z, col = me_e // 2, me_e % 2
    pos = z + col * (n - 1 - 2 * z)

    def at(place):
        place = (place + n) % n
        upper = place // half
        return 2 * place + upper * (2 * n - 1 - 4 * place)

    right = (me_g, at(pos + 1), me_d)
    left = (me_g, at(pos - 1), me_d)
    mate = (me_g, me_e, 1 - me_d)

    loads = [
        pltpu.make_async_copy(src, dst, w_sem.at[i])
        for i, (src, dst) in enumerate(((wg_hbm, wg), (wu_hbm, wu), (wd_hbm, wd)))
    ]
    for load in loads:
        load.start()

    barrier = pltpu.get_barrier_semaphore()
    for other in (left, right, mate):
        pl.semaphore_signal(barrier, inc=1, device_id=other, device_id_type=MESH)
    xs[pl.ds(0, rows), :] = x_in[...]
    cs[pl.ds(0, rows), :] = c_in[...]
    pl.semaphore_wait(barrier, 3)

    def slot(way, t):
        if t == 0:
            return 0
        if t == half:
            return n - 1
        return 2 * t - 1 + way

    def gather(way, arr, t):
        buf = (xs, cs)[arr]
        return pltpu.make_async_remote_copy(
            src_ref=buf.at[pl.ds(slot(way, t - 1) * rows, rows)],
            dst_ref=buf.at[pl.ds(slot(way, t) * rows, rows)],
            send_sem=g_send.at[way, arr, t - 1],
            recv_sem=g_recv.at[way, arr, t - 1],
            device_id=(right, left)[way],
            device_id_type=MESH,
        )

    def moves(t):
        if t < half:
            return [gather(0, 0, t), gather(1, 0, t), gather(0, 1, t), gather(1, 1, t)]
        return [gather(0, 0, t), gather(1, 1, t)]

    started = []

    def advance(t):
        later = {0: moves(t + 1)} if t < half else {0: []}
        if t == 0:
            for move in later[0]:
                move.start()
        elif t < half - 1:
            for now, move in zip(moves(t), later[0]):
                now.wait_recv()
                move.start()
        elif t == half - 1:
            now = moves(t)
            now[0].wait_recv()
            later[0][0].start()
            now[3].wait_recv()
            later[0][1].start()
            now[1].wait_recv()
            now[2].wait_recv()
        else:
            for now in moves(t):
                now.wait_recv()
        started.extend(later[0])

    early = (n // 4) * 2 + 1
    spans = ((0, early * rows), (early * rows, (n - early) * rows))

    def swap(chunk, j):
        span = pl.ds(*spans[chunk])
        return pltpu.make_async_remote_copy(
            src_ref=snd.at[j, :, span],
            dst_ref=rcv.at[j, :, span],
            send_sem=d_send.at[chunk, j],
            recv_sem=d_recv.at[chunk, j],
            device_id=mate,
            device_id_type=MESH,
        )

    def project(chunk):
        span = pl.ds(*spans[chunk])

        def body(j, carry):
            for m, value in enumerate((
                lambda: dot(xs[span, :], wg[j], NN),
                lambda: dot(xs[span, :], wu[j], NN),
                lambda: dot(cs[span, pl.ds(0, width)], wd[j], NT),
            )):
                result = value()
                own[j, m, span] = result
                snd[j, m, span] = result.astype(BF16)
            swap(chunk, j).start()
            return carry

        lax.fori_loop(0, local, body, 0)

    def activate(chunk):
        first, count = spans[chunk]
        span = pl.ds(first, count)

        def body(j, carry):
            swap(chunk, j).wait_recv()
            tail = cs[span, pl.ds(width, cs.shape[1] - width)].astype(F32)
            lane = lax.broadcasted_iota(jnp.int32, tail.shape, 1)
            mine = me_e * local + j
            p = jnp.sum(
                jnp.where((lane == mine) | (lane == mine + experts), tail, 0.0), axis=1, keepdims=True
            )
            gate = own[j, 0, span] + rcv[j, 0, span].astype(F32)
            up = own[j, 1, span] + rcv[j, 1, span].astype(F32)
            back = p * (own[j, 2, span] + rcv[j, 2, span].astype(F32))
            sig = jax.nn.sigmoid(gate)
            act = gate * sig
            hid[j, span] = (p * (act * up)).astype(BF16)
            gat[j, span] = (back * up * sig * (1.0 + gate * (1.0 - sig))).astype(BF16)
            upg[j, span] = (back * act).astype(BF16)
            return carry

        lax.fori_loop(0, local, body, 0)

    def combine(chunk):
        span = pl.ds(*spans[chunk])
        part[0, span] = dot(hid[0, span], wd[0], NN)
        part[1, span] = dot(gat[0, span], wg[0], NT) + dot(upg[0, span], wu[0], NT)

        def body(j, carry):
            part[0, span] += dot(hid[j, span], wd[j], NN)
            part[1, span] += dot(gat[j, span], wg[j], NT) + dot(upg[j, span], wu[j], NT)
            return carry

        lax.fori_loop(1, local, body, 0)

    for t in range(n // 4 + 1):
        advance(t)
    for load in loads:
        load.wait()
    project(0)
    for t in range(n // 4 + 1, half):
        advance(t)
    activate(0)
    combine(0)
    advance(half)
    project(1)
    xt[...] = xs[...].T
    activate(1)
    combine(1)

    def ring(way, arr, d):
        return pltpu.make_async_remote_copy(
            src_ref=red_out.at[way, arr, d - 1],
            dst_ref=red_in.at[way, arr, d - 1],
            send_sem=r_send.at[way, arr, d - 1],
            recv_sem=r_recv.at[way, arr, d - 1],
            device_id=(right, left)[way],
            device_id_type=MESH,
        )

    def forward(way, arr, d):
        value = part[arr, pl.ds(slot(1 - way, d) * rows, rows)]
        if d < half - 1 or (d == half - 1 and arr == way):
            ring(way, arr, d + 1).wait_recv()
            value = value + red_in[way, arr, d].astype(F32)
        red_out[way, arr, d - 1] = value.astype(BF16)
        move = ring(way, arr, d)
        move.start()
        started.append(move)

    writes = []

    def weight_grad(j, kind):
        buf, hbm = ((out_g, gg_hbm), (out_u, gu_hbm), (out_d, gd_hbm))[kind]
        if kind == 0:
            buf[j] = dot(xt[...], gat[j], NN).astype(BF16)
        elif kind == 1:
            buf[j] = dot(xt[...], upg[j], NN).astype(BF16)
        else:
            buf[j] = dot(hid[j], cs[:, pl.ds(0, width)], TN).astype(BF16)
        copy = pltpu.make_async_copy(buf.at[j], hbm.at[j], o_sem.at[kind, j])
        copy.start()
        writes.append(copy)

    jobs = [(j, kind) for j in range(local) for kind in range(3)]
    ticks = [(0, half)]
    for d in range(half - 1, 0, -1):
        ticks += [(1, d), (0, d)]
    for i, (arr, d) in enumerate(ticks):
        forward(0, arr, d)
        forward(1, 1 - arr, d)
        if i >= 1:
            take = -(-len(jobs) // (len(ticks) - i))
            for job in jobs[:take]:
                weight_grad(*job)
            jobs = jobs[take:]

    for arr, ref in ((0, moe_ref), (1, gn_ref)):
        total = part[arr, pl.ds(0, rows)]
        for way in range(2):
            ring(way, arr, 1).wait_recv()
            total = total + red_in[way, arr, 0].astype(F32)
        ref[...] = total.astype(BF16)

    for move in started:
        move.wait_send()
    for chunk in range(2):
        for j in range(local):
            swap(chunk, j).wait_send()
    for copy in writes:
        copy.wait()


def fused(normed, cotangent, routes, w_gate, w_up, w_down):
    tok_rows, width = normed.shape
    local, _, hidden = w_gate.shape
    n = lax.axis_size("expert")
    experts = routes.shape[1]
    rows = -(-tok_rows // 16) * 16
    pad = rows - tok_rows
    tail = -(-2 * experts // 128) * 128
    high = lax.reduce_precision(routes, 8, 7)
    coded = jnp.concatenate([high, routes - high], axis=1).astype(BF16)
    coded = jnp.pad(coded, ((0, pad), (0, tail - 2 * experts)))
    x_in = jnp.pad(normed, ((0, pad), (0, 0)))
    c_in = jnp.concatenate([jnp.pad(cotangent, ((0, pad), (0, 0))), coded], axis=1)
    total, half = n * rows, n // 2
    any_spec, vmem_spec = pl.BlockSpec(memory_space=pl.ANY), pl.BlockSpec(memory_space=pltpu.VMEM)
    dma = pltpu.SemaphoreType.DMA
    moe, grad, gg, gu, gd = pl.pallas_call(
        functools.partial(kernel, n, rows, width, experts),
        out_shape=(
            jax.ShapeDtypeStruct((rows, width), BF16),
            jax.ShapeDtypeStruct((rows, width), BF16),
            jax.ShapeDtypeStruct(w_gate.shape, BF16),
            jax.ShapeDtypeStruct(w_up.shape, BF16),
            jax.ShapeDtypeStruct(w_down.shape, BF16),
        ),
        in_specs=[vmem_spec, vmem_spec, any_spec, any_spec, any_spec],
        out_specs=(vmem_spec, vmem_spec, any_spec, any_spec, any_spec),
        scratch_shapes=[
            pltpu.VMEM((total, width), BF16),
            pltpu.VMEM((total, width + tail), BF16),
            pltpu.VMEM((width, total), BF16),
            pltpu.VMEM(w_gate.shape, BF16),
            pltpu.VMEM(w_up.shape, BF16),
            pltpu.VMEM(w_down.shape, BF16),
            pltpu.VMEM((local, 3, total, hidden), F32),
            pltpu.VMEM((local, 3, total, hidden), BF16),
            pltpu.VMEM((local, 3, total, hidden), BF16),
            pltpu.VMEM((local, total, hidden), BF16),
            pltpu.VMEM((local, total, hidden), BF16),
            pltpu.VMEM((local, total, hidden), BF16),
            pltpu.VMEM((2, total, width), F32),
            pltpu.VMEM((2, 2, half, rows, width), BF16),
            pltpu.VMEM((2, 2, half, rows, width), BF16),
            pltpu.VMEM(w_gate.shape, BF16),
            pltpu.VMEM(w_up.shape, BF16),
            pltpu.VMEM(w_down.shape, BF16),
            dma((3,)),
            dma((2, 2, half)),
            dma((2, 2, half)),
            dma((2, local)),
            dma((2, local)),
            dma((2, 2, half)),
            dma((2, 2, half)),
            dma((3, local)),
        ],
        compiler_params=pltpu.CompilerParams(
            collective_id=0, has_side_effects=True, vmem_limit_bytes=60 * 2**20
        ),
    )(x_in, c_in, w_gate, w_up, w_down)
    return moe[:tok_rows], grad[:tok_rows], gg, gu, gd


def plain(normed, cotangent, routes, w_gate, w_up, w_down):
    local = w_gate.shape[0]
    rows = lax.all_gather(normed, "expert", axis=0, tiled=True)
    grads = lax.all_gather(cotangent, "expert", axis=0, tiled=True)
    probs = lax.all_gather(routes, "expert", axis=0, tiled=True)
    probs = lax.dynamic_slice_in_dim(probs, lax.axis_index("expert") * local, local, axis=1)
    p = probs.T[:, :, None]
    ein = functools.partial(jnp.einsum, preferred_element_type=F32)
    gate, up, back = lax.psum(
        (ein("rd,jdf->jrf", rows, w_gate), ein("rd,jdf->jrf", rows, w_up), ein("rd,jfd->jrf", grads, w_down)),
        "dp",
    )
    back = p * back
    sig = jax.nn.sigmoid(gate)
    act = gate * sig
    hid = (p * (act * up)).astype(BF16)
    gat = (back * up * sig * (1.0 + gate * (1.0 - sig))).astype(BF16)
    upg = (back * act).astype(BF16)
    moe = ein("jrf,jfd->rd", hid, w_down)
    grad = ein("jrf,jdf->rd", gat, w_gate) + ein("jrf,jdf->rd", upg, w_up)
    return (
        lax.psum_scatter(moe, "expert", scatter_dimension=0, tiled=True).astype(BF16),
        lax.psum_scatter(grad, "expert", scatter_dimension=0, tiled=True).astype(BF16),
        ein("rd,jrf->jdf", rows, gat).astype(BF16),
        ein("rd,jrf->jdf", rows, upg).astype(BF16),
        ein("jrf,rd->jfd", hid, grads).astype(BF16),
    )


def shards(normed, cotangent, expert_ids, route_weights, w_gate, w_up, w_down):
    n, pair = lax.axis_size("expert"), lax.axis_size("dp")
    experts = w_gate.shape[0] * n
    chosen = expert_ids[:, :, None] == jnp.arange(experts, dtype=jnp.int32)[None, None, :]
    routes = jnp.sum(jnp.where(chosen, route_weights[:, :, None], 0.0), axis=1)
    form = fused if pair == 2 and 4 <= n <= 8 and n % 4 == 0 else plain
    return form(normed, cotangent, routes, w_gate, w_up, w_down)


def solution(mesh):
    in_specs = (
        P(("groups", "expert"), "dp"),
        P(("groups", "expert"), "dp"),
        P(("groups", "expert"), None),
        P(("groups", "expert"), None),
        P("expert", "dp", None),
        P("expert", "dp", None),
        P("expert", None, "dp"),
    )
    out_specs = (
        P(("groups", "expert"), "dp"),
        P(("groups", "expert"), "dp"),
        P(("groups", "expert"), "dp", None),
        P(("groups", "expert"), "dp", None),
        P(("groups", "expert"), None, "dp"),
    )
    return jax.shard_map(shards, mesh=mesh, in_specs=in_specs, out_specs=out_specs, check_vma=False)
```

time: 270 us -> 68.3 us (0.25)
  waiting for transfers between devices: 134 us -> 0 us
  Pallas kernels: 0 us -> 51.5 us
  local copies, waits for them, and re-layouts: 62.2 us -> 13.4 us
  matrix products: 23.8 us -> 0 us
  starting transfers between devices: 22.1 us -> 0 us
  between operations: 14.3 us -> 0.65 us
  other arithmetic: 12.6 us -> 2.39 us
    all_to_all x4 -> x0, waiting for transfers between devices: 106 us -> none  [the longest x1 37.3 us: shards(): lax.all_to_all(out_rows[None], 'expert', split_axis=2, concat_axis=0, til...]
    pallas_call x0 -> x1, Pallas kernels: none -> 51.5 us  [fused(): pl.pallas_call(functools.partial(kernel, n, rows, width, experts), out_sh...]
    psum x1 -> x0, waiting for transfers between devices: 27.8 us -> none  [shards(): pre_gate, pre_up = lax.psum((part_gate, part_up), 'dp')]
    dot_general x9 -> x0, matrix products: 23.8 us -> none  [the longest x1 4.44 us: shards(): jnp.einsum('jrd,jdf->jrf', rows, up_all, preferred_element_type=jnp.float32)]
    all_to_all x4 -> x0, starting transfers between devices: 22 us -> none  [the longest x1 7.38 us: shards(): lax.all_to_all(send_rows, 'expert', split_axis=0, concat_axis=2, tiled=True)]
    gather x4 -> x0, local copies, waits for them, and re-layouts: 17.1 us -> none  [the longest x1 5.75 us: shards(): send_grads = g_padded[table].reshape(count_dev, local_experts, slots, width)]
    unnamed x30 -> x9, local copies, waits for them, and re-layouts: 0.96 us -> 11.7 us
    reshape x5 -> x0, local copies, waits for them, and re-layouts: 10.3 us -> none  [the longest x1 3.06 us: shards(): x_padded[token_of].reshape(count_dev, local_experts, slots, width)]
  transfers between devices with their start and end apart: 5 -> 0, of which waited for: 5 -> 0; matrix products, arithmetic and copies ran while one was open for 20% -> 0% of each run, Pallas kernels for 0% -> 0%
where the time goes in v1:
time: 68.3 us; the launch traced here: 68 us
  Pallas kernels  51.5 us (75%)
  local copies, waits for them, and re-layouts  13.4 us (20%)
  other arithmetic  2.39 us (3%)
    pallas_call x1, Pallas kernels, fused(): pl.pallas_call(functools.partial(kernel, n, rows, width, experts), out_sh...  51.5 us
    unnamed x9, local copies, waits for them, and re-layouts  11.7 us
    concatenate x1, other arithmetic, fused(): jnp.concatenate([jnp.pad(cotangent, ((0, pad), (0, 0))), coded], axis=1)  1.55 us
    pad x1, local copies, waits for them, and re-layouts, fused(): x_in = jnp.pad(normed, ((0, pad), (0, 0)))  1.54 us

profile of v1, /device:TPU:0, one launch (start us, length us, event | category | flops | bytes accessed | tf_op | source)
XLA Modules:
  0.0 68.0 jit_solution(6121358861385609919)
XLA Ops:
  0.6 0.7 %select_reduce_fusion = f32[42,24]{0,1:T(8,128)S(1)} fusion(f32[42,10]{0,1:T(8,128)} %param.10, s32[42,10]{0,1:T(8,128)} %param.9), kind=kLoop, calls=%fused_computation.2 | loop fusion | flops 29232 | bytes 7392 | tf_op jit(solution)/shard_map/reduce_sum | solution.py:342
  1.4 0.1 copy.17
  1.5 0.1 copy.16
  1.6 0.1 fusion.7
  1.7 1.6 %fusion.1.c_in = bf16[48,1152]{1,0:T(8,128)(2,1)} fusion(bf16[42,1024]{1,0:T(8,128)(2,1)} %param.8, bf16[48,128]{1,0:T(8,128)(2,1)S(1)} %fusion.7), kind=kLoop, calls=%fused_computation.4 | loop fusion | flops 331776 | bytes 208896 | tf_op jit(solution)/shard_map/concatenate | solution.py:259
  3.2 1.5 %pad.11.x_in = bf16[48,1024]{1,0:T(8,128)(2,1)} pad(bf16[42,1024]{1,0:T(8,128)(2,1)} %param.7, bf16[]{:T(256)} %constant.1.clone.1), padding=0_6x0_0 | pad | bytes 184322 | tf_op jit(solution)/shard_map/jit(_pad)/pad | solution.py:258
  4.8 51.5 %shard_map.110 = (bf16[48,1024]{1,0:T(8,128)(2,1)}, bf16[48,1024]{1,0:T(8,128)(2,1)}, bf16[3,1024,512]{2,1,0:T(8,128)(2,1)}, bf16[3,1024,512]{2,1,0:T(8,128)(2,1)}, bf16[3,512,1024]{2,1,0:T(8,128)(2,1)}) custom-call(bf16[48,1024]{1,0:T(8,128)(2,1)} %pad.11.x_in, bf16[48,1152]{1,0:T(8,128)(2,1)} %fusion.1.c_in, bf16[3,1024,512]{2,1,0:T(8,128)(2,1)} %wg_hbm.1, ...), custom_call_target="tpu_custom_call" | custom-call | tf_op jit(solution)/shard_map/pallas_call | solution.py:263
  56.3 1.5 %copy.24 = bf16[42,1024]{1,0:T(8,128)(2,1)} copy(bf16[42,1024]{1,0:T(8,128)(2,1)} %bitcast.3) | data formatting | bytes 172032
  57.8 1.5 %copy.25 = bf16[42,1024]{1,0:T(8,128)(2,1)} copy(bf16[42,1024]{1,0:T(8,128)(2,1)} %bitcast.2) | data formatting | bytes 172032
  59.3 0.0 copy-start.1
  59.3 3.9 %copy.26 = bf16[3,1024,512]{2,1,0:T(8,128)(2,1)} copy(bf16[3,1024,512]{2,1,0:T(8,128)(2,1)} %get-tuple-element.24) | data formatting | bytes 6291456
  63.3 0.0 copy-done.1
  63.3 0.0 copy-start
  63.3 1.7 %copy.27 = bf16[3,1024,512]{2,1,0:T(8,128)(2,1)} copy(bf16[3,1024,512]{2,1,0:T(8,128)(2,1)S(1)} %copy-done.1) | data formatting | bytes 6291456
  64.9 1.4 %copy-done = bf16[3,512,1024]{2,1,0:T(8,128)(2,1)S(1)} copy-done((bf16[3,512,1024]{2,1,0:T(8,128)(2,1)S(1)}, bf16[3,512,1024]{2,1,0:T(8,128)(2,1)}, u32[]{:S(2)}) %copy-start) | copy-done | bytes 3145752
  66.3 1.7 %copy.28 = bf16[3,512,1024]{2,1,0:T(8,128)(2,1)} copy(bf16[3,512,1024]{2,1,0:T(8,128)(2,1)S(1)} %copy-done) | data formatting | bytes 6291456
  (2 shorter events, 0.0 us)
Async XLA Ops:
  59.3 3.9 %copy-start.1 = (bf16[3,1024,512]{2,1,0:T(8,128)(2,1)S(1)}, bf16[3,1024,512]{2,1,0:T(8,128)(2,1)}, u32[]{:S(2)}) copy-start(bf16[3,1024,512]{2,1,0:T(8,128)(2,1)} %get-tuple-element.25) | copy-start | bytes 9437188
  63.3 3.0 %copy-start = (bf16[3,512,1024]{2,1,0:T(8,128)(2,1)S(1)}, bf16[3,512,1024]{2,1,0:T(8,128)(2,1)}, u32[]{:S(2)}) copy-start(bf16[3,512,1024]{2,1,0:T(8,128)(2,1)} %get-tuple-element.26) | copy-start | bytes 9437188

commit v2 on v1

--- a/solution.py
+++ b/solution.py
@@ -18,11 +18,10 @@
     return lax.dot_general(a, b, dims, preferred_element_type=F32)
 
 
-def kernel(n, rows, width, experts, x_in, c_in, wg_hbm, wu_hbm, wd_hbm,
-           moe_ref, gn_ref, gg_hbm, gu_hbm, gd_hbm,
+def kernel(n, rows, width, experts, x_in, c_in, ids, weights, wg_hbm, wu_hbm, wd_hbm,
+           moe_ref, gn_ref, gg_ref, gu_ref, gd_ref,
            xs, cs, xt, wg, wu, wd, own, snd, rcv, hid, gat, upg, part, red_out, red_in,
-           out_g, out_u, out_d,
-           w_sem, g_send, g_recv, d_send, d_recv, r_send, r_recv, o_sem):
+           w_sem, g_send, g_recv, d_send, d_recv, r_send, r_recv):
     half = n // 2
     local = wg.shape[0]
     me_g, me_e, me_d = lax.axis_index("groups"), lax.axis_index("expert"), lax.axis_index("dp")
@@ -48,8 +47,24 @@
     barrier = pltpu.get_barrier_semaphore()
     for other in (left, right, mate):
         pl.semaphore_signal(barrier, inc=1, device_id=other, device_id_type=MESH)
-    xs[pl.ds(0, rows), :] = x_in[...]
-    cs[pl.ds(0, rows), :] = c_in[...]
+    tokens = x_in.shape[0]
+    if rows > tokens:
+        part[:, pl.ds(tokens, rows - tokens), :] = jnp.zeros((2, rows - tokens, width), F32)
+    part[0, pl.ds(0, tokens), :] = x_in[...].astype(F32)
+    part[1, pl.ds(0, tokens), :] = c_in[...].astype(F32)
+    xs[pl.ds(0, rows), :] = part[0, pl.ds(0, rows), :].astype(BF16)
+    cs[pl.ds(0, rows), pl.ds(0, width)] = part[1, pl.ds(0, rows), :].astype(BF16)
+    tail = cs.shape[1] - width
+    place = lax.broadcasted_iota(jnp.int32, (tail, tokens), 0)
+    high, low = jnp.zeros((tail, tokens), F32), jnp.zeros((tail, tokens), F32)
+    for k in range(ids.shape[0]):
+        name, weight = ids[pl.ds(k, 1), :], weights[pl.ds(k, 1), :]
+        high = high + jnp.where(place == name, weight, 0.0)
+        low = low + jnp.where(place == name + experts, weight, 0.0)
+    low = low - low.astype(BF16).astype(F32)
+    part[0, pl.ds(0, tail), pl.ds(0, 128)] = jnp.zeros((tail, 128), F32)
+    part[0, pl.ds(0, tail), pl.ds(0, tokens)] = high + low
+    cs[pl.ds(0, rows), pl.ds(width, tail)] = part[0, pl.ds(0, tail), pl.ds(0, 128)].T[:rows].astype(BF16)
     pl.semaphore_wait(barrier, 3)
 
     def slot(way, t):
@@ -201,19 +216,14 @@
         move.start()
         started.append(move)
 
-    writes = []
-
     def weight_grad(j, kind):
-        buf, hbm = ((out_g, gg_hbm), (out_u, gu_hbm), (out_d, gd_hbm))[kind]
+        buf = (gg_ref, gu_ref, gd_ref)[kind]
         if kind == 0:
             buf[j] = dot(xt[...], gat[j], NN).astype(BF16)
         elif kind == 1:
             buf[j] = dot(xt[...], upg[j], NN).astype(BF16)
         else:
             buf[j] = dot(hid[j], cs[:, pl.ds(0, width)], TN).astype(BF16)
-        copy = pltpu.make_async_copy(buf.at[j], hbm.at[j], o_sem.at[kind, j])
-        copy.start()
-        writes.append(copy)
 
     jobs = [(j, kind) for j in range(local) for kind in range(3)]
     ticks = [(0, half)]
@@ -233,44 +243,51 @@
         for way in range(2):
             ring(way, arr, 1).wait_recv()
             total = total + red_in[way, arr, 0].astype(F32)
-        ref[...] = total.astype(BF16)
+        part[arr, pl.ds(0, rows)] = total
+        ref[...] = part[arr, pl.ds(0, tokens)].astype(BF16)
 
     for move in started:
         move.wait_send()
     for chunk in range(2):
         for j in range(local):
             swap(chunk, j).wait_send()
-    for copy in writes:
+
+
+def deliver(moe, grad, gg, gu, gd, moe_out, grad_out, gg_out, gu_out, gd_out, sem):
+    copies = [
+        pltpu.make_async_copy(src.at[j], dst.at[j], sem.at[i, j])
+        for i, (src, dst) in enumerate(((gg, gg_out), (gu, gu_out), (gd, gd_out)))
+        for j in range(src.shape[0])
+    ]
+    for copy in copies:
+        copy.start()
+    moe_out[...] = moe[...]
+    grad_out[...] = grad[...]
+    for copy in copies:
         copy.wait()
 
 
-def fused(normed, cotangent, routes, w_gate, w_up, w_down):
+def fused(normed, cotangent, expert_ids, route_weights, w_gate, w_up, w_down):
     tok_rows, width = normed.shape
     local, _, hidden = w_gate.shape
     n = lax.axis_size("expert")
-    experts = routes.shape[1]
+    experts = local * n
     rows = -(-tok_rows // 16) * 16
-    pad = rows - tok_rows
     tail = -(-2 * experts // 128) * 128
-    high = lax.reduce_precision(routes, 8, 7)
-    coded = jnp.concatenate([high, routes - high], axis=1).astype(BF16)
-    coded = jnp.pad(coded, ((0, pad), (0, tail - 2 * experts)))
-    x_in = jnp.pad(normed, ((0, pad), (0, 0)))
-    c_in = jnp.concatenate([jnp.pad(cotangent, ((0, pad), (0, 0))), coded], axis=1)
     total, half = n * rows, n // 2
     any_spec, vmem_spec = pl.BlockSpec(memory_space=pl.ANY), pl.BlockSpec(memory_space=pltpu.VMEM)
     dma = pltpu.SemaphoreType.DMA
     moe, grad, gg, gu, gd = pl.pallas_call(
         functools.partial(kernel, n, rows, width, experts),
         out_shape=(
-            jax.ShapeDtypeStruct((rows, width), BF16),
-            jax.ShapeDtypeStruct((rows, width), BF16),
-            jax.ShapeDtypeStruct(w_gate.shape, BF16),
-            jax.ShapeDtypeStruct(w_up.shape, BF16),
-            jax.ShapeDtypeStruct(w_down.shape, BF16),
+            pltpu.VMEM((tok_rows, width), BF16),
+            pltpu.VMEM((tok_rows, width), BF16),
+            pltpu.VMEM(w_gate.shape, BF16),
+            pltpu.VMEM(w_up.shape, BF16),
+            pltpu.VMEM(w_down.shape, BF16),
         ),
-        in_specs=[vmem_spec, vmem_spec, any_spec, any_spec, any_spec],
-        out_specs=(vmem_spec, vmem_spec, any_spec, any_spec, any_spec),
+        in_specs=[vmem_spec, vmem_spec, vmem_spec, vmem_spec, any_spec, any_spec, any_spec],
+        out_specs=(vmem_spec, vmem_spec, vmem_spec, vmem_spec, vmem_spec),
         scratch_shapes=[
             pltpu.VMEM((total, width), BF16),
             pltpu.VMEM((total, width + tail), BF16),
@@ -287,9 +304,6 @@
             pltpu.VMEM((2, total, width), F32),
             pltpu.VMEM((2, 2, half, rows, width), BF16),
             pltpu.VMEM((2, 2, half, rows, width), BF16),
-            pltpu.VMEM(w_gate.shape, BF16),
-            pltpu.VMEM(w_up.shape, BF16),
-            pltpu.VMEM(w_down.shape, BF16),
             dma((3,)),
             dma((2, 2, half)),
             dma((2, 2, half)),
@@ -297,13 +311,21 @@
             dma((2, local)),
             dma((2, 2, half)),
             dma((2, 2, half)),
-            dma((3, local)),
         ],
         compiler_params=pltpu.CompilerParams(
-            collective_id=0, has_side_effects=True, vmem_limit_bytes=60 * 2**20
+            collective_id=0, has_side_effects=True, vmem_limit_bytes=46 * 2**20
         ),
-    )(x_in, c_in, w_gate, w_up, w_down)
-    return moe[:tok_rows], grad[:tok_rows], gg, gu, gd
+    )(normed, cotangent, expert_ids.T, route_weights.T, w_gate, w_up, w_down)
+    moe, grad, gg, gu, gd = (pltpu.with_memory_space_constraint(a, pltpu.VMEM) for a in (moe, grad, gg, gu, gd))
+    shapes = tuple(jax.ShapeDtypeStruct(a.shape, BF16) for a in (moe, grad, gg, gu, gd))
+    return pl.pallas_call(
+        deliver,
+        out_shape=shapes,
+        in_specs=[vmem_spec] * 5,
+        out_specs=(vmem_spec, vmem_spec, any_spec, any_spec, any_spec),
+        scratch_shapes=[dma((3, local))],
+        compiler_params=pltpu.CompilerParams(vmem_limit_bytes=4 * 2**20),
+    )(moe, grad, gg, gu, gd)
 
 
 def plain(normed, cotangent, routes, w_gate, w_up, w_down):
@@ -338,10 +360,11 @@
 def shards(normed, cotangent, expert_ids, route_weights, w_gate, w_up, w_down):
     n, pair = lax.axis_size("expert"), lax.axis_size("dp")
     experts = w_gate.shape[0] * n
+    if pair == 2 and 4 <= n <= 8 and n % 4 == 0:
+        return fused(normed, cotangent, expert_ids, route_weights, w_gate, w_up, w_down)
     chosen = expert_ids[:, :, None] == jnp.arange(experts, dtype=jnp.int32)[None, None, :]
     routes = jnp.sum(jnp.where(chosen, route_weights[:, :, None], 0.0), axis=1)
-    form = fused if pair == 2 and 4 <= n <= 8 and n % 4 == 0 else plain
-    return form(normed, cotangent, routes, w_gate, w_up, w_down)
+    return plain(normed, cotangent, routes, w_gate, w_up, w_down)
 
 
 def solution(mesh):

time: 68.3 us -> 55.9 us (0.82)
  local copies, waits for them, and re-layouts: 13.4 us -> 0 us
  Pallas kernels: 51.5 us -> 55.1 us
  other arithmetic: 2.39 us -> 0 us
    unnamed x9 -> x0, local copies, waits for them, and re-layouts: 11.7 us -> none
    pallas_call x0 -> x1, Pallas kernels: none -> 4.37 us  [fused(): pl.pallas_call(deliver, out_shape=shapes, in_specs=[vmem_spec] * 5, out_s...]
    concatenate x2 -> x0, other arithmetic: 1.64 us -> none  [the longest x1 1.55 us: fused(): jnp.concatenate([jnp.pad(cotangent, ((0, pad), (0, 0))), coded], axis=1)]
    pad x1 -> x0, local copies, waits for them, and re-layouts: 1.54 us -> none  [fused(): x_in = jnp.pad(normed, ((0, pad), (0, 0)))]
    pallas_call x1, Pallas kernels: 51.5 us -> 50.7 us  [fused(): pl.pallas_call(functools.partial(kernel, n, rows, width, experts), out_sh...]
    reduce_sum x1 -> x0, other arithmetic: 0.74 us -> none  [shards(): routes = jnp.sum(jnp.where(chosen, route_weights[:, :, None], 0.0), axis=1)]
where the time goes in v2:
time: 55.9 us; the launch traced here: 55.8 us
  Pallas kernels  55.1 us (99%)
  between operations  0.64 us (1%)
    pallas_call x1, Pallas kernels, fused(): pl.pallas_call(functools.partial(kernel, n, rows, width, experts), out_sh...  50.7 us
    pallas_call x1, Pallas kernels, fused(): pl.pallas_call(deliver, out_shape=shapes, in_specs=[vmem_spec] * 5, out_s...  4.37 us

profile of v2, /device:TPU:0, one launch (start us, length us, event | category | flops | bytes accessed | tf_op | source)
XLA Modules:
  0.0 55.8 jit_solution(640194118999236093)
XLA Ops:
  0.6 50.7 %shard_map.110 = (bf16[42,1024]{1,0:T(8,128)(2,1)S(1)}, bf16[42,1024]{1,0:T(8,128)(2,1)S(1)}, bf16[3,1024,512]{2,1,0:T(8,128)(2,1)S(1)}, bf16[3,1024,512]{2,1,0:T(8,128)(2,1)S(1)}, bf16[3,512,1024]{2,1,0:T(8,128)(2,1)S(1)}) custom-call(bf16[42,1024]{1,0:T(8,128)(2,1)} %x_in.1, bf16[42,1024]{1,0:T(8,128)(2,1)} %c_in.1, s32[10,42]{1,0:T(8,128)} %bitcast.2, ...), custom_call_target="tpu_custom_call" | custom-call | tf_op jit(solution)/shard_map/pallas_call | solution.py:280
  51.4 4.4 %shard_map.111 = (bf16[42,1024]{1,0:T(8,128)(2,1)}, bf16[42,1024]{1,0:T(8,128)(2,1)}, bf16[3,1024,512]{2,1,0:T(8,128)(2,1)}, bf16[3,1024,512]{2,1,0:T(8,128)(2,1)}, bf16[3,512,1024]{2,1,0:T(8,128)(2,1)}) custom-call(bf16[42,1024]{1,0:T(8,128)(2,1)S(1)} %get-tuple-element.10.moe, bf16[42,1024]{1,0:T(8,128)(2,1)S(1)} %get-tuple-element.11.grad, ...), custom_call_target="tpu_custom_call" | custom-call | tf_op jit(solution)/shard_map/pallas_call | solution.py:321

commit v3 on v2

--- a/solution.py
+++ b/solution.py
@@ -24,6 +24,9 @@
            w_sem, g_send, g_recv, d_send, d_recv, r_send, r_recv):
     half = n // 2
     local = wg.shape[0]
+    cut = rows * 2 // 3 // 16 * 16
+    sizes, offsets, bases = (cut, rows - cut), (0, cut), (0, n * cut)
+    spans = ((0, n * cut), (n * cut, n * (rows - cut)))
     me_g, me_e, me_d = lax.axis_index("groups"), lax.axis_index("expert"), lax.axis_index("dp")
     z, col = me_e // 2, me_e % 2
     pos = z + col * (n - 1 - 2 * z)
@@ -52,8 +55,9 @@
         part[:, pl.ds(tokens, rows - tokens), :] = jnp.zeros((2, rows - tokens, width), F32)
     part[0, pl.ds(0, tokens), :] = x_in[...].astype(F32)
     part[1, pl.ds(0, tokens), :] = c_in[...].astype(F32)
-    xs[pl.ds(0, rows), :] = part[0, pl.ds(0, rows), :].astype(BF16)
-    cs[pl.ds(0, rows), pl.ds(0, width)] = part[1, pl.ds(0, rows), :].astype(BF16)
+    for size, offset, base in zip(sizes, offsets, bases):
+        xs[pl.ds(base, size), :] = part[0, pl.ds(offset, size), :].astype(BF16)
+        cs[pl.ds(base, size), pl.ds(0, width)] = part[1, pl.ds(offset, size), :].astype(BF16)
     tail = cs.shape[1] - width
     place = lax.broadcasted_iota(jnp.int32, (tail, tokens), 0)
     high, low = jnp.zeros((tail, tokens), F32), jnp.zeros((tail, tokens), F32)
@@ -64,7 +68,9 @@
     low = low - low.astype(BF16).astype(F32)
     part[0, pl.ds(0, tail), pl.ds(0, 128)] = jnp.zeros((tail, 128), F32)
     part[0, pl.ds(0, tail), pl.ds(0, tokens)] = high + low
-    cs[pl.ds(0, rows), pl.ds(width, tail)] = part[0, pl.ds(0, tail), pl.ds(0, 128)].T[:rows].astype(BF16)
+    coded = part[0, pl.ds(0, tail), pl.ds(0, 128)].T
+    for size, offset, base in zip(sizes, offsets, bases):
+        cs[pl.ds(base, size), pl.ds(width, tail)] = coded[offset:offset + size].astype(BF16)
     pl.semaphore_wait(barrier, 3)
 
     def slot(way, t):
@@ -74,48 +80,46 @@
             return n - 1
         return 2 * t - 1 + way
 
-    def gather(way, arr, t):
+    def gather(phase, way, arr, t):
+        base, size = bases[phase], sizes[phase]
         buf = (xs, cs)[arr]
         return pltpu.make_async_remote_copy(
-            src_ref=buf.at[pl.ds(slot(way, t - 1) * rows, rows)],
-            dst_ref=buf.at[pl.ds(slot(way, t) * rows, rows)],
-            send_sem=g_send.at[way, arr, t - 1],
-            recv_sem=g_recv.at[way, arr, t - 1],
+            src_ref=buf.at[pl.ds(base + slot(way, t - 1) * size, size)],
+            dst_ref=buf.at[pl.ds(base + slot(way, t) * size, size)],
+            send_sem=g_send.at[phase, way, arr, t - 1],
+            recv_sem=g_recv.at[phase, way, arr, t - 1],
             device_id=(right, left)[way],
             device_id_type=MESH,
         )
 
-    def moves(t):
+    def moves(phase, t):
         if t < half:
-            return [gather(0, 0, t), gather(1, 0, t), gather(0, 1, t), gather(1, 1, t)]
-        return [gather(0, 0, t), gather(1, 1, t)]
+            return [gather(phase, way, arr, t) for arr in range(2) for way in range(2)]
+        return [gather(phase, 0, 0, t), gather(phase, 1, 1, t)]
 
     started = []
 
-    def advance(t):
-        later = {0: moves(t + 1)} if t < half else {0: []}
+    def advance(phase, t):
+        now = moves(phase, t) if t > 0 else []
+        later = moves(phase, t + 1) if t < half else []
+        started.extend(later)
         if t == 0:
-            for move in later[0]:
+            for move in later:
                 move.start()
         elif t < half - 1:
-            for now, move in zip(moves(t), later[0]):
-                now.wait_recv()
+            for arrived, move in zip(now, later):
+                arrived.wait_recv()
                 move.start()
         elif t == half - 1:
-            now = moves(t)
             now[0].wait_recv()
-            later[0][0].start()
+            later[0].start()
             now[3].wait_recv()
-            later[0][1].start()
+            later[1].start()
             now[1].wait_recv()
             now[2].wait_recv()
         else:
-            for now in moves(t):
-                now.wait_recv()
-        started.extend(later[0])
-
-    early = (n // 4) * 2 + 1
-    spans = ((0, early * rows), (early * rows, (n - early) * rows))
+            for arrived in now:
+                arrived.wait_recv()
 
     def swap(chunk, j):
         span = pl.ds(*spans[chunk])
@@ -181,40 +185,38 @@
 
         lax.fori_loop(1, local, body, 0)
 
-    for t in range(n // 4 + 1):
-        advance(t)
-    for load in loads:
-        load.wait()
-    project(0)
-    for t in range(n // 4 + 1, half):
-        advance(t)
-    activate(0)
-    combine(0)
-    advance(half)
-    project(1)
-    xt[...] = xs[...].T
-    activate(1)
-    combine(1)
-
-    def ring(way, arr, d):
+    def ring(phase, way, arr, d):
+        span = pl.ds(offsets[phase], sizes[phase])
         return pltpu.make_async_remote_copy(
-            src_ref=red_out.at[way, arr, d - 1],
-            dst_ref=red_in.at[way, arr, d - 1],
-            send_sem=r_send.at[way, arr, d - 1],
-            recv_sem=r_recv.at[way, arr, d - 1],
+            src_ref=red_out.at[way, arr, d - 1, span],
+            dst_ref=red_in.at[way, arr, d - 1, span],
+            send_sem=r_send.at[phase, way, arr, d - 1],
+            recv_sem=r_recv.at[phase, way, arr, d - 1],
             device_id=(right, left)[way],
             device_id_type=MESH,
         )
 
-    def forward(way, arr, d):
-        value = part[arr, pl.ds(slot(1 - way, d) * rows, rows)]
+    def forward(phase, way, arr, d):
+        size, span = sizes[phase], pl.ds(offsets[phase], sizes[phase])
+        value = part[arr, pl.ds(bases[phase] + slot(1 - way, d) * size, size)]
         if d < half - 1 or (d == half - 1 and arr == way):
-            ring(way, arr, d + 1).wait_recv()
-            value = value + red_in[way, arr, d].astype(F32)
-        red_out[way, arr, d - 1] = value.astype(BF16)
-        move = ring(way, arr, d)
+            ring(phase, way, arr, d + 1).wait_recv()
+            value = value + red_in[way, arr, d, span].astype(F32)
+        red_out[way, arr, d - 1, span] = value.astype(BF16)
+        move = ring(phase, way, arr, d)
         move.start()
         started.append(move)
+
+    ticks = [(0, half)]
+    for d in range(half - 1, 0, -1):
+        ticks += [(1, d), (0, d)]
+    waiting = [list(ticks), list(ticks)]
+
+    def tick(phase, count=1):
+        for arr, d in waiting[phase][:count]:
+            forward(phase, 0, arr, d)
+            forward(phase, 1, 1 - arr, d)
+        waiting[phase] = waiting[phase][count:]
 
     def weight_grad(j, kind):
         buf = (gg_ref, gu_ref, gd_ref)[kind]
@@ -225,25 +227,44 @@
         else:
             buf[j] = dot(hid[j], cs[:, pl.ds(0, width)], TN).astype(BF16)
 
+    advance(0, 0)
+    for t in range(1, half):
+        advance(0, t)
+        advance(1, t - 1)
+    advance(0, half)
+    for load in loads:
+        load.wait()
+    project(0)
+    advance(1, half - 1)
+    activate(0)
+    combine(0)
+    tick(0, 2)
+    advance(1, half)
+    project(1)
+    tick(0)
+    xt[...] = xs[...].T
+    tick(0)
+    activate(1)
+    tick(0)
+    combine(1)
+    tick(1, 2)
     jobs = [(j, kind) for j in range(local) for kind in range(3)]
-    ticks = [(0, half)]
-    for d in range(half - 1, 0, -1):
-        ticks += [(1, d), (0, d)]
-    for i, (arr, d) in enumerate(ticks):
-        forward(0, arr, d)
-        forward(1, 1 - arr, d)
-        if i >= 1:
-            take = -(-len(jobs) // (len(ticks) - i))
-            for job in jobs[:take]:
-                weight_grad(*job)
-            jobs = jobs[take:]
+    while jobs or waiting[0] or waiting[1]:
+        tick(0)
+        left_ticks = max(1, len(waiting[1]))
+        for job in jobs[:-(-len(jobs) // left_ticks)]:
+            weight_grad(*job)
+        jobs = jobs[-(-len(jobs) // left_ticks):]
+        tick(1)
 
     for arr, ref in ((0, moe_ref), (1, gn_ref)):
-        total = part[arr, pl.ds(0, rows)]
-        for way in range(2):
-            ring(way, arr, 1).wait_recv()
-            total = total + red_in[way, arr, 0].astype(F32)
-        part[arr, pl.ds(0, rows)] = total
+        for phase in range(2):
+            span = pl.ds(offsets[phase], sizes[phase])
+            total = part[arr, pl.ds(bases[phase], sizes[phase])]
+            for way in range(2):
+                ring(phase, way, arr, 1).wait_recv()
+                total = total + red_in[way, arr, 0, span].astype(F32)
+            part[arr, span] = total
         ref[...] = part[arr, pl.ds(0, tokens)].astype(BF16)
 
     for move in started:
@@ -305,12 +326,12 @@
             pltpu.VMEM((2, 2, half, rows, width), BF16),
             pltpu.VMEM((2, 2, half, rows, width), BF16),
             dma((3,)),
-            dma((2, 2, half)),
-            dma((2, 2, half)),
+            dma((2, 2, 2, half)),
+            dma((2, 2, 2, half)),
             dma((2, local)),
             dma((2, local)),
-            dma((2, 2, half)),
-            dma((2, 2, half)),
+            dma((2, 2, 2, half)),
+            dma((2, 2, 2, half)),
         ],
         compiler_params=pltpu.CompilerParams(
             collective_id=0, has_side_effects=True, vmem_limit_bytes=46 * 2**20
@@ -360,7 +381,7 @@
 def shards(normed, cotangent, expert_ids, route_weights, w_gate, w_up, w_down):
     n, pair = lax.axis_size("expert"), lax.axis_size("dp")
     experts = w_gate.shape[0] * n
-    if pair == 2 and 4 <= n <= 8 and n % 4 == 0:
+    if pair == 2 and 4 <= n <= 8 and n % 4 == 0 and 16 < normed.shape[0] <= 128:
         return fused(normed, cotangent, expert_ids, route_weights, w_gate, w_up, w_down)
     chosen = expert_ids[:, :, None] == jnp.arange(experts, dtype=jnp.int32)[None, None, :]
     routes = jnp.sum(jnp.where(chosen, route_weights[:, :, None], 0.0), axis=1)

time: 55.9 us -> 58 us (1.038)
  Pallas kernels: 55.1 us -> 57.2 us
    pallas_call x1, Pallas kernels: 50.7 us -> 52.8 us  [fused(): pl.pallas_call(functools.partial(kernel, n, rows, width, experts), out_sh...]
where the time goes in v3:
time: 58 us; the launch traced here: 57.8 us
  Pallas kernels  57.2 us (99%)
  between operations  0.64 us (1%)
    pallas_call x1, Pallas kernels, fused(): pl.pallas_call(functools.partial(kernel, n, rows, width, experts), out_sh...  52.8 us
    pallas_call x1, Pallas kernels, fused(): pl.pallas_call(deliver, out_shape=shapes, in_specs=[vmem_spec] * 5, out_s...  4.37 us

profile of v3, /device:TPU:0, one launch (start us, length us, event | category | flops | bytes accessed | tf_op | source)
XLA Modules:
  0.0 57.8 jit_solution(6411724768285848130)
XLA Ops:
  0.6 52.8 %shard_map.110 = (bf16[42,1024]{1,0:T(8,128)(2,1)S(1)}, bf16[42,1024]{1,0:T(8,128)(2,1)S(1)}, bf16[3,1024,512]{2,1,0:T(8,128)(2,1)S(1)}, bf16[3,1024,512]{2,1,0:T(8,128)(2,1)S(1)}, bf16[3,512,1024]{2,1,0:T(8,128)(2,1)S(1)}) custom-call(bf16[42,1024]{1,0:T(8,128)(2,1)} %x_in.1, bf16[42,1024]{1,0:T(8,128)(2,1)} %c_in.1, s32[10,42]{1,0:T(8,128)} %bitcast.2, ...), custom_call_target="tpu_custom_call" | custom-call | tf_op jit(solution)/shard_map/pallas_call | solution.py:301
  53.4 4.4 %shard_map.111 = (bf16[42,1024]{1,0:T(8,128)(2,1)}, bf16[42,1024]{1,0:T(8,128)(2,1)}, bf16[3,1024,512]{2,1,0:T(8,128)(2,1)}, bf16[3,1024,512]{2,1,0:T(8,128)(2,1)}, bf16[3,512,1024]{2,1,0:T(8,128)(2,1)}) custom-call(bf16[42,1024]{1,0:T(8,128)(2,1)S(1)} %get-tuple-element.10.moe, bf16[42,1024]{1,0:T(8,128)(2,1)S(1)} %get-tuple-element.11.grad, ...), custom_call_target="tpu_custom_call" | custom-call | tf_op jit(solution)/shard_map/pallas_call | solution.py:342

commit v4 on v2

--- a/solution.py
+++ b/solution.py
@@ -131,7 +131,7 @@
     def project(chunk):
         span = pl.ds(*spans[chunk])
 
-        def body(j, carry):
+        def body(j):
             for m, value in enumerate((
                 lambda: dot(xs[span, :], wg[j], NN),
                 lambda: dot(xs[span, :], wu[j], NN),
@@ -141,15 +141,15 @@
                 own[j, m, span] = result
                 snd[j, m, span] = result.astype(BF16)
             swap(chunk, j).start()
-            return carry
-
-        lax.fori_loop(0, local, body, 0)
+
+        for j in range(local):
+            body(j)
 
     def activate(chunk):
         first, count = spans[chunk]
         span = pl.ds(first, count)
 
-        def body(j, carry):
+        def body(j):
             swap(chunk, j).wait_recv()
             tail = cs[span, pl.ds(width, cs.shape[1] - width)].astype(F32)
             lane = lax.broadcasted_iota(jnp.int32, tail.shape, 1)
@@ -165,21 +165,16 @@
             hid[j, span] = (p * (act * up)).astype(BF16)
             gat[j, span] = (back * up * sig * (1.0 + gate * (1.0 - sig))).astype(BF16)
             upg[j, span] = (back * act).astype(BF16)
-            return carry
-
-        lax.fori_loop(0, local, body, 0)
+
+        for j in range(local):
+            body(j)
 
     def combine(chunk):
         span = pl.ds(*spans[chunk])
-        part[0, span] = dot(hid[0, span], wd[0], NN)
-        part[1, span] = dot(gat[0, span], wg[0], NT) + dot(upg[0, span], wu[0], NT)
-
-        def body(j, carry):
-            part[0, span] += dot(hid[j, span], wd[j], NN)
-            part[1, span] += dot(gat[j, span], wg[j], NT) + dot(upg[j, span], wu[j], NT)
-            return carry
-
-        lax.fori_loop(1, local, body, 0)
+        part[0, span] = sum(dot(hid[j, span], wd[j], NN) for j in range(local))
+        part[1, span] = sum(
+            dot(gat[j, span], wg[j], NT) + dot(upg[j, span], wu[j], NT) for j in range(local)
+        )
 
     for t in range(n // 4 + 1):
         advance(t)

time: 55.9 us -> 54.6 us (0.977)
  Pallas kernels: 55.1 us -> 53.8 us
    pallas_call x1, Pallas kernels: 50.7 us -> 49.5 us  [fused(): pl.pallas_call(functools.partial(kernel, n, rows, width, experts), out_sh...]
where the time goes in v4:
time: 54.6 us; the launch traced here: 54.5 us
  Pallas kernels  53.8 us (99%)
  between operations  0.64 us (1%)
    pallas_call x1, Pallas kernels, fused(): pl.pallas_call(functools.partial(kernel, n, rows, width, experts), out_sh...  49.5 us
    pallas_call x1, Pallas kernels, fused(): pl.pallas_call(deliver, out_shape=shapes, in_specs=[vmem_spec] * 5, out_s...  4.37 us

profile of v4, /device:TPU:0, one launch (start us, length us, event | category | flops | bytes accessed | tf_op | source)
XLA Modules:
  0.0 54.5 jit_solution(12211528434470919072)
XLA Ops:
  0.6 49.5 %shard_map.110 = (bf16[42,1024]{1,0:T(8,128)(2,1)S(1)}, bf16[42,1024]{1,0:T(8,128)(2,1)S(1)}, bf16[3,1024,512]{2,1,0:T(8,128)(2,1)S(1)}, bf16[3,1024,512]{2,1,0:T(8,128)(2,1)S(1)}, bf16[3,512,1024]{2,1,0:T(8,128)(2,1)S(1)}) custom-call(bf16[42,1024]{1,0:T(8,128)(2,1)} %x_in.1, bf16[42,1024]{1,0:T(8,128)(2,1)} %c_in.1, s32[10,42]{1,0:T(8,128)} %bitcast.2, ...), custom_call_target="tpu_custom_call" | custom-call | tf_op jit(solution)/shard_map/pallas_call | solution.py:275
  50.1 4.4 %shard_map.111 = (bf16[42,1024]{1,0:T(8,128)(2,1)}, bf16[42,1024]{1,0:T(8,128)(2,1)}, bf16[3,1024,512]{2,1,0:T(8,128)(2,1)}, bf16[3,1024,512]{2,1,0:T(8,128)(2,1)}, bf16[3,512,1024]{2,1,0:T(8,128)(2,1)}) custom-call(bf16[42,1024]{1,0:T(8,128)(2,1)S(1)} %get-tuple-element.10.moe, bf16[42,1024]{1,0:T(8,128)(2,1)S(1)} %get-tuple-element.11.grad, ...), custom_call_target="tpu_custom_call" | custom-call | tf_op jit(solution)/shard_map/pallas_call | solution.py:316
